TPU v7x, 32 devices: a whole 2x2x4 slice. The times are simulated.
32 devices in a mesh: rep: 8 (over y, x, core), tp: 4 (over z).
Axes of the slice: x: 2, y: 2, z: 4, core: 2. Of those that a mesh axis runs over, the one named last changes fastest.
Arguments:
- hidden: bfloat16 [36864, 1024], P('rep', 'tp'), may hold values from -0.09375 to 0.09375
- out_grad: bfloat16 [36864, 512], P(('rep', 'tp')), may hold values from -6 to 6
- momentum: float32 [8, 1024, 512], P('rep', 'tp'), may hold values from -6 to 6
- band_rows: int32 [16, 8], P('tp'), may hold values from 0 to 48, as said below
- band_start_columns: int32 [16, 8], P('tp'), may hold values from 0 to 48, as said below
Outputs:
- momentum_out: float32 [8, 1024, 512], P('rep', 'tp')
- update: bfloat16 [1024, 512], P('tp')
Inputs may be any that keep to these rules, and one draw needn't show every extreme that they name: `band_rows`: multiples of 16, the same for every replica. `band_start_columns`: multiples of 16, the same for every replica.
All inputs are finite; a program needn't handle non-finite values.
Results may differ from a plain program's by a relative error of at most 0.001.
Values may be sent and summed in bfloat16 or wider, within the bound.
No kernel may reach another device: no remote copies, remote signals or barrier semaphores. Data moves between devices by JAX's collectives and lax.ppermute only.
A program may use at most 64 MiB of HBM per device.

v0:
```python
import jax
import jax.numpy as jnp
from jax import lax
from jax.sharding import PartitionSpec as P

decay_rate = 0.9
highest_precision = lax.Precision.HIGHEST


def band_basis(offsets):
    frequency = (offsets.reshape(-1, 1, 1) + jnp.arange(16, dtype=jnp.int32)[None, :, None]).astype(
        jnp.float32
    )
    sample_pos = jnp.arange(64, dtype=jnp.float32)[None, None, :]
    norm_scale = jnp.where(
        frequency == 0, jnp.sqrt(jnp.float32(1.0 / 64)), jnp.sqrt(jnp.float32(2.0 / 64))
    )
    return norm_scale * jnp.cos(jnp.pi * (sample_pos + 0.5) * frequency / 64)


def local(hidden, out_grad, momentum, band_rows, band_start_columns):
    row_count = hidden.shape[1]
    col_count = out_grad.shape[1]
    group_rows = row_count // 64
    group_cols = col_count // 64
    row_cosine_matrix = band_basis(band_rows)
    column_cosine_matrix = band_basis(band_start_columns)

    def from_blocks(blocks):
        return (
            blocks.reshape(group_rows, group_cols, 64, 64)
            .transpose(0, 2, 1, 3)
            .reshape(row_count, col_count)
        )

    def lift(frequency_bands):
        return jnp.einsum(
            "cji,cjk,ckl->cil",
            row_cosine_matrix,
            frequency_bands,
            column_cosine_matrix,
            precision=highest_precision,
        )

    carried_over = decay_rate * momentum[0]
    gradient = lax.dot_general(
        hidden,
        lax.all_gather(out_grad, "tp", axis=0, tiled=True),
        (((0,), (0,)), ((), ())),
        preferred_element_type=jnp.float32,
    )
    combined_blocks = (
        (carried_over + gradient)
        .reshape(group_rows, 64, group_cols, 64)
        .transpose(0, 2, 1, 3)
        .reshape(group_rows * group_cols, 64, 64)
    )
    frequency_bands = jnp.einsum(
        "hag,hgt,hbt->hab",
        row_cosine_matrix,
        combined_blocks,
        column_cosine_matrix,
        precision=highest_precision,
    )
    momentum_out = from_blocks(combined_blocks - lift(frequency_bands))
    summed = lax.psum(frequency_bands, "rep")
    update = from_blocks(lift(summed)).astype(jnp.bfloat16)
    return (momentum_out[None], update)


def solution(mesh):
    return jax.shard_map(
        local,
        mesh=mesh,
        in_specs=(
            P("rep", "tp"),
            P(("rep", "tp"), None),
            P("rep", "tp", None),
            P("tp", None),
            P("tp", None),
        ),
        out_specs=(P("rep", "tp", None), P("tp", None)),
        check_vma=False,
    )
```

profile of v0, /device:TPU:0, one launch (start us, length us, event | category | flops | bytes accessed | tf_op | source)
XLA Modules:
  0.0 161.4 jit_solution(2691085235469570756)
XLA Ops:
  7.2 0.0 copy-start
  7.2 0.0 all-gather.2.cloned.1.call-start
  7.2 0.7 all-gather.2.cloned.1.call-update
  7.9 0.8 add.63
  8.7 0.8 add.68
  9.4 0.1 compare_select_fusion
  9.5 0.1 add_convert_fusion
  9.6 0.1 compare_select_fusion.1
  9.7 0.1 add_convert_fusion.1
  9.7 92.0 %all-gather.2.cloned.1.call-done = bf16[4608,512]{1,0:T(8,128)(2,1)} async-done(((bf16[1152,512]{1,0:T(8,128)(2,1)}), bf16[4608,512]{1,0:T(8,128)(2,1)}) %all-gather.2.cloned.1.call-update) | async-done | bytes 4718608 | tf_op jit(solution)/shard_map/all_gather | solution.py:48
  101.7 0.0 copy-done
  101.7 3.9 %convolution_add_fusion = f32[256,512]{1,0:T(8,128)S(1)} fusion(bf16[4608,256]{1,0:T(8,128)(2,1)S(1)} %copy-done, bf16[4608,512]{1,0:T(8,128)(2,1)} %all-gather.2.cloned.1.call-done, f32[1,256,512]{2,1,0:T(8,128)} %param.7), kind=kOutput, calls=%fused_computation.2 | convolution fusion | flops 1208221696 | bytes 8126464 | tf_op jit(solution)/shard_map/dot_general | solution.py:46
  105.6 1.2 reshape.138
  106.8 1.4 copy.7
  108.2 2.0 %fusion.3 = f32[32,64,16]{1,2,0:T(8,128)S(1)} fusion(f32[32,64,64]{2,1,0:T(8,128)S(1)} %bitcast.22, f32[32,16]{1,0:T(8,128)S(1)} %add_convert_fusion.1, f32[64]{0:T(128)S(1)} %add_multiply_fusion, f32[32,16]{1,0:T(8,128)S(1)} %compare_select_fusion.1), kind=kOutput, calls=%fused_computation.8 | convolution fusion | flops 25264128 | bytes 659712 | tf_op jit(solution)/shard_map/hag,hgt,hbt->hab/dot_general | solution.py:58
  110.2 2.2 %fusion = f32[32,16,16]{2,1,0:T(8,128)} fusion(f32[32,64,16]{1,2,0:T(8,128)S(1)} %fusion.3, f32[32,16]{1,0:T(8,128)S(1)} %add_convert_fusion, f32[32,16]{1,0:T(8,128)S(1)} %compare_select_fusion, f32[64]{0:T(128)S(1)} %add_multiply_fusion), kind=kOutput, calls=%fused_computation.4 | convolution fusion | flops 6389760 | bytes 168192 | tf_op jit(solution)/shard_map/hag,hgt,hbt->hab/dot_general | solution.py:58
  112.4 28.1 %psum.7 = f32[32,16,16]{2,1,0:T(8,128)} all-reduce(f32[32,16,16]{2,1,0:T(8,128)} %fusion), channel_id=1, replica_groups=mesh['rep'=8,'tp'=4] {'rep'}, use_global_device_ids=true, to_apply=%region_0.1 | all-reduce | flops 8192 | bytes 65536 | tf_op jit(solution)/shard_map/psum | solution.py:66
  140.6 0.0 copy-start.1
  140.6 2.4 %fusion.2 = f32[32,16,64]{2,1,0:T(8,128)S(1)} fusion(f32[32,16,16]{2,1,0:T(8,128)} %fusion, f32[32,16]{1,0:T(8,128)S(1)} %add_convert_fusion.1, f32[64]{0:T(128)S(1)} %add_multiply_fusion, f32[32,16]{1,0:T(8,128)S(1)} %compare_select_fusion.1), kind=kOutput, calls=%fused_computation.7 | convolution fusion | flops 6389760 | bytes 168192 | tf_op jit(solution)/shard_map/cji,cjk,ckl->cil/dot_general | solution.py:37
  143.0 2.7 %convolution_subtract_fusion = f32[32,64,64]{2,1,0:T(8,128)S(1)} fusion(f32[32,64,64]{2,1,0:T(8,128)S(1)} %bitcast.23, f32[32,16,64]{2,1,0:T(8,128)S(1)} %fusion.2, f32[32,16]{1,0:T(8,128)S(1)} %add_convert_fusion, f32[32,16]{1,0:T(8,128)S(1)} %compare_select_fusion, f32[64]{0:T(128)S(1)} %add_multiply_fusion), kind=kOutput, calls=%fused_computation | convolution fusion | flops 25395200 | bytes 1184000 | tf_op jit(solution)/shard_map/cji,cjk,ckl->cil/dot_general | solution.py:37
  145.7 0.0 copy-done.1
  145.7 2.2 %fusion.1 = f32[32,16,64]{2,1,0:T(8,128)} fusion(f32[32,16,16]{2,1,0:T(8,128)S(1)} %copy-done.1, f32[32,16]{1,0:T(8,128)S(1)} %add_convert_fusion.1, f32[64]{0:T(128)S(1)} %add_multiply_fusion, f32[32,16]{1,0:T(8,128)S(1)} %compare_select_fusion.1), kind=kOutput, calls=%fused_computation.6 | convolution fusion | flops 6389760 | bytes 168192 | tf_op jit(solution)/shard_map/cji,cjk,ckl->cil/dot_general | solution.py:37
  147.9 0.6 copy.8
  148.5 1.1 broadcast_in_dim_reshape.3
  149.5 3.6 %convolution_convert_fusion = bf16[32,64,64]{2,1,0:T(8,128)(2,1)S(1)} fusion(f32[32,16,64]{2,1,0:T(8,128)} %fusion.1, f32[32,16]{1,0:T(8,128)S(1)} %add_convert_fusion, f32[32,16]{1,0:T(8,128)S(1)} %compare_select_fusion, f32[64]{0:T(128)S(1)} %add_multiply_fusion), kind=kOutput, calls=%fused_computation.1 | convolution fusion | flops 25395200 | bytes 397568 | tf_op jit(solution)/shard_map/cji,cjk,ckl->cil/dot_general | solution.py:37
  153.1 0.3 copy.9
  153.5 1.0 convert_element_type.39
  (1 shorter events, 0.0 us)
Async XLA Ops:
  7.2 94.6 %copy-start = (bf16[4608,256]{1,0:T(8,128)(2,1)S(1)}, bf16[4608,256]{1,0:T(8,128)(2,1)}, u32[]{:S(2)}) copy-start(bf16[4608,256]{1,0:T(8,128)(2,1)} %param.5) | copy-start | bytes 7077892
  7.2 94.5 %all-gather.2.cloned.1.call-start = ((), (), s32[]{:S(2)}) async-start(), calls=%async_computation | async-start | bytes 5898240 | tf_op jit(solution)/shard_map/all_gather | solution.py:48
  140.6 5.1 %copy-start.1 = (f32[32,16,16]{2,1,0:T(8,128)S(1)}, f32[32,16,16]{2,1,0:T(8,128)}, u32[]{:S(2)}) copy-start(f32[32,16,16]{2,1,0:T(8,128)} %psum.7) | copy-start | bytes 98308
Sparse Core Ops, SparseCore 0:
  9.6 92.0 all-gather.1
where the time goes:
time: 162 us; the launch traced here: 161 us
  waiting for transfers between devices  92.7 us (57%)
  blocking collectives  28.1 us (17%)
  matrix products  19 us (12%)
  between operations  14.1 us (9%)
  local copies, waits for them, and re-layouts  7.19 us (4%)
    all_gather x1, waiting for transfers between devices, local(): lax.all_gather(out_grad, 'tp', axis=0, tiled=True)  92 us
    psum x1, blocking collectives, local(): summed = lax.psum(frequency_bands, 'rep')  28.1 us
    dot_general x4, matrix products, lift(): jnp.einsum('cji,cjk,ckl->cil', row_cosine_matrix, frequency_bands, column...  10.9 us
    dot_general x2, matrix products, local(): jnp.einsum('hag,hgt,hbt->hab', row_cosine_matrix, combined_blocks, column...  4.23 us
    dot_general x1, matrix products, local(): lax.dot_general(hidden, lax.all_gather(out_grad, 'tp', axis=0, tiled=True...  3.86 us
  transfers between devices with their start and end apart: 1, of which 1 were waited for; matrix products, arithmetic and copies ran while one was open for 1% of the time, Pallas kernels for 0%

commit v1 on v0

v1 whole, which is shorter than its diff:
```python
import functools

import jax
import jax.numpy as jnp
import numpy as np
from jax import lax
from jax.experimental import pallas as pl
from jax.experimental.pallas import tpu as pltpu
from jax.sharding import PartitionSpec as P

decay_rate = 0.9
order = 64
band = 16
steps = order // band


def basis_matrix():
    frequency = np.arange(order, dtype=np.float64)[:, None]
    sample_pos = np.arange(order, dtype=np.float64)[None, :]
    norm_scale = np.where(frequency == 0, np.sqrt(1.0 / order), np.sqrt(2.0 / order))
    return norm_scale * np.cos(np.pi * (sample_pos + 0.5) * frequency / order)


def halves_of(matrix):
    high = matrix.astype(jnp.bfloat16)
    low = (matrix - high.astype(matrix.dtype)).astype(jnp.bfloat16)
    return np.stack([high, low])


def diagonal_blocks(width):
    count = next(c for c in (4, 2, 1) if width % (c * order) == 0)
    return halves_of(np.kron(np.eye(count), basis_matrix()))


def fold_matrix(width):
    return np.kron(np.eye(width // order), np.kron(np.ones((steps, 1)), np.eye(band))).astype(jnp.bfloat16)


def split2(x):
    high = x.astype(jnp.bfloat16)
    return high, (x - high.astype(jnp.float32)).astype(jnp.bfloat16)


def split3(x):
    high, low = split2(x)
    rest = x - high.astype(jnp.float32) - low.astype(jnp.float32)
    return high, low, rest.astype(jnp.bfloat16)


def dot(a, b, dims=((1,), (0,))):
    return lax.dot_general(a, b, (dims, ((), ())), preferred_element_type=jnp.float32)


def dot3(a, b, dims=((1,), (0,))):
    return dot(a[0], b[0], dims) + (dot(a[0], b[1], dims) + dot(a[1], b[0], dims))


def on_rows(basis_ref, x, transposed):
    basis = basis_ref[0], basis_ref[1]
    side = basis[0].shape[0]
    dims = ((0,), (0,)) if transposed else ((1,), (0,))
    parts = [dot3(basis, split2(x[i : i + side]), dims) for i in range(0, x.shape[0], side)]
    return parts[0] if len(parts) == 1 else jnp.concatenate(parts, axis=0)


def on_columns(basis_ref, x, transposed):
    basis = basis_ref[0], basis_ref[1]
    side = basis[0].shape[0]
    dims = ((1,), (0,)) if transposed else ((1,), (1,))
    parts = [dot3(split2(x[:, i : i + side]), basis, dims) for i in range(0, x.shape[1], side)]
    return parts[0] if len(parts) == 1 else jnp.concatenate(parts, axis=1)


def column_mask(row, cols_ref, width):
    group = lax.rem(lax.broadcasted_iota(jnp.int32, (band, width), 1), order) // band
    return group == cols_ref[row : row + 1, :]


def lifted(folded, rows_ref, cols_ref, fold_ref, row_basis_ref, column_basis_ref):
    width = cols_ref.shape[1]
    spread = sum(dot(part, fold_ref[...], ((1,), (1,))) for part in split3(folded))
    pieces = []
    for row in range(rows_ref.shape[0]):
        inside = jnp.where(column_mask(row, cols_ref, width), spread[row * band : (row + 1) * band], 0.0)
        for step in range(steps):
            pieces.append(jnp.where(rows_ref[row : row + 1, :] == step, inside, 0.0))
    coefficients = jnp.concatenate(pieces, axis=0)
    return on_columns(column_basis_ref, on_rows(row_basis_ref, coefficients, True), True)


def bands_kernel(m_ref, rows_ref, cols_ref, fold_ref, row_basis_ref, column_basis_ref, bands_ref):
    width = cols_ref.shape[1]
    coefficients = on_columns(column_basis_ref, on_rows(row_basis_ref, m_ref[...], False), False)
    pieces = []
    for row in range(rows_ref.shape[0]):
        taken = jnp.zeros((band, width), jnp.float32)
        for step in range(steps):
            at = row * order + step * band
            taken = jnp.where(rows_ref[row : row + 1, :] == step, coefficients[at : at + band], taken)
        pieces.append(jnp.where(column_mask(row, cols_ref, width), taken, 0.0))
    taken = jnp.concatenate(pieces, axis=0)
    bands_ref[...] = sum(dot(part, fold_ref[...]) for part in split3(taken))


def remove_kernel(m_ref, bands_ref, rows_ref, cols_ref, fold_ref, row_basis_ref, column_basis_ref, out_ref):
    out_ref[...] = m_ref[...] - lifted(
        bands_ref[...], rows_ref, cols_ref, fold_ref, row_basis_ref, column_basis_ref
    )


def update_kernel(*refs):
    *part_refs, rows_ref, cols_ref, fold_ref, row_basis_ref, column_basis_ref, out_ref = refs
    parts = [ref[...] for ref in part_refs]
    out_ref[...] = lifted(
        pair_sum(parts), rows_ref, cols_ref, fold_ref, row_basis_ref, column_basis_ref
    ).astype(out_ref.dtype)


def pair_sum(parts):
    while len(parts) > 1:
        parts = [a + b for a, b in zip(parts[::2], parts[1::2])]
    return parts[0]


def call(kernel, shape, dtype, *operands):
    return pl.pallas_call(
        kernel,
        out_shape=jax.ShapeDtypeStruct(shape, dtype),
        compiler_params=pltpu.CompilerParams(vmem_limit_bytes=32 * 2**20),
        cost_estimate=pl.CostEstimate(
            flops=4 * 10**8, bytes_accessed=4 * 10**6, transcendentals=0
        ),
    )(*operands)


def spread_sum(x, axis):
    size = lax.axis_size(axis)
    if size & (size - 1):
        return [lax.psum(x, axis)]
    stride, parts = 1, [x]
    while stride < size:
        count = min(8, size // stride)
        x = pair_sum(parts)
        parts = [x] + [
            lax.ppermute(x, axis, [(i, i ^ (stride * k)) for i in range(size)]) for k in range(1, count)
        ]
        stride *= count
    return parts


def product(hidden_rows, grad_rows):
    return dot(hidden_rows, grad_rows, ((0,), (0,)))


def gathered_gradient(hidden, out_grad):
    return product(hidden, lax.all_gather(out_grad, "tp", axis=0, tiled=True))


def line_gradient(hidden, out_grad):
    tok = out_grad.shape[0]
    me = lax.axis_index("tp")
    left = me < 2
    pair = me ^ 1
    cross = jnp.where(left, 2, 1)
    far = jnp.where(left, 3, 0)

    def rows_of(part):
        return lax.dynamic_slice_in_dim(hidden, part * tok, tok, 0)

    def send(x, perm):
        return lax.ppermute(x, "tp", perm)

    both_ways = [(0, 1), (1, 0), (2, 3), (3, 2)]
    across = [(1, 2), (2, 1)]
    outward = [(1, 0), (2, 3)]
    inward = [(0, 1), (3, 2)]

    pair_grad = send(out_grad, both_ways)
    cross_grad = send(out_grad, across)
    far_hidden = rows_of(far)
    sent_hidden, pair_grad = lax.optimization_barrier((far_hidden, pair_grad))
    far_grad = send(pair_grad, across)
    cross_grad = cross_grad + send(cross_grad, outward)
    helped_hidden = send(sent_hidden, inward)
    helped = send(product(helped_hidden, far_grad), outward)
    gradient = product(rows_of(me), out_grad) + product(rows_of(pair), pair_grad)
    gradient = gradient + product(rows_of(cross), cross_grad)
    return gradient + product(far_hidden, far_grad) + helped


def local(hidden, out_grad, momentum, band_rows, band_start_columns):
    row_count = hidden.shape[1]
    col_count = out_grad.shape[1]
    rows = jnp.repeat(band_rows.astype(jnp.int32) // band, order, axis=1)
    cols = jnp.repeat(band_start_columns.astype(jnp.int32) // band, order, axis=1)
    tables = (
        rows,
        cols,
        jnp.asarray(fold_matrix(col_count)),
        jnp.asarray(diagonal_blocks(row_count)),
        jnp.asarray(diagonal_blocks(col_count)),
    )
    gradient = (line_gradient if lax.axis_size("tp") == 4 else gathered_gradient)(hidden, out_grad)
    m = decay_rate * momentum[0] + gradient
    folded_shape = (row_count // steps, col_count // steps)
    bands = call(bands_kernel, folded_shape, jnp.float32, m, *tables)
    parts = spread_sum(bands, "rep")
    momentum_out = call(remove_kernel, m.shape, jnp.float32, m, bands, *tables)
    update = call(update_kernel, m.shape, jnp.bfloat16, *parts, *tables)
    return (momentum_out[None], update)


def solution(mesh):
    return jax.shard_map(
        local,
        mesh=mesh,
        in_specs=(
            P("rep", "tp"),
            P(("rep", "tp"), None),
            P("rep", "tp", None),
            P("tp", None),
            P("tp", None),
        ),
        out_specs=(P("rep", "tp", None), P("tp", None)),
        check_vma=False,
    )
```

time: 162 us -> 92.6 us (0.57)
  waiting for transfers between devices: 92.7 us -> 52.4 us
  blocking collectives: 28.1 us -> 0 us
  starting transfers between devices: 0.04 us -> 21.8 us
  between operations: 14.1 us -> 0.83 us
  matrix products: 19 us -> 9.01 us
  Pallas kernels: 0 us -> 4.24 us
  local copies, waits for them, and re-layouts: 7.19 us -> 3.83 us
    all_gather x1 -> x0, waiting for transfers between devices: 92 us -> none  [local(): lax.all_gather(out_grad, 'tp', axis=0, tiled=True)]
    ppermute x0 -> x13, waiting for transfers between devices: none -> 52.4 us  [the longest x6 50.9 us: send(): return lax.ppermute(x, 'tp', perm)]
    psum x1 -> x0, blocking collectives: 28.1 us -> none  [local(): summed = lax.psum(frequency_bands, 'rep')]
    ppermute x0 -> x13, starting transfers between devices: none -> 21.8 us  [the longest x6 15.3 us: send(): return lax.ppermute(x, 'tp', perm)]
    dot_general x7 -> x5, matrix products: 19 us -> 9.01 us  [dot(): lax.dot_general(a, b, (dims, ((), ())), preferred_element_type=jnp.float32)]
    pallas_call x0 -> x3, Pallas kernels: none -> 4.24 us  [call(): pl.pallas_call(kernel, out_shape=jax.ShapeDtypeStruct(shape, dtype), comp...]
    transpose x2 -> x0, local copies, waits for them, and re-layouts: 2.02 us -> none  [the longest x1 1.41 us: local(): combined_blocks = (carried_over + gradient).reshape(group_rows, 64, group...]
  transfers between devices with their start and end apart: 1 -> 13, of which waited for: 1 -> 6; matrix products, arithmetic and copies ran while one was open for 1% -> 12% of each run, Pallas kernels for 0% -> 2%
where the time goes in v1:
time: 92.6 us; the launch traced here: 92.1 us
  waiting for transfers between devices  52.4 us (57%)
  starting transfers between devices  21.8 us (24%)
  matrix products  9.01 us (10%)
  Pallas kernels  4.24 us (5%)
  local copies, waits for them, and re-layouts  3.83 us (4%)
    ppermute x6, waiting for transfers between devices, send(): return lax.ppermute(x, 'tp', perm)  50.9 us
    ppermute x6, starting transfers between devices, send(): return lax.ppermute(x, 'tp', perm)  15.3 us
    dot_general x5, matrix products, dot(): lax.dot_general(a, b, (dims, ((), ())), preferred_element_type=jnp.float32)  9.01 us
    ppermute x7, starting transfers between devices, spread_sum(): lax.ppermute(x, axis, [(i, i ^ stride * k) for i in range(size)])  6.47 us
    pallas_call x3, Pallas kernels, call(): pl.pallas_call(kernel, out_shape=jax.ShapeDtypeStruct(shape, dtype), comp...  4.24 us
  transfers between devices with their start and end apart: 13, of which 6 were waited for; matrix products, arithmetic and copies ran while one was open for 12% of the time, Pallas kernels for 2%

profile of v1, /device:TPU:0, one launch (start us, length us, event | category | flops | bytes accessed | tf_op | source)
XLA Modules:
  0.0 92.1 jit_solution(1914808076860340516)
XLA Ops:
  0.6 0.0 copy-start
  0.6 0.0 copy-start.4
  0.7 0.0 copy-start.5
  0.7 3.1 %collective-permute-start = (bf16[1152,512]{1,0:T(8,128)(2,1)}, bf16[1152,512]{1,0:T(8,128)(2,1)}, u32[]{:S(2)}, u32[]{:S(2)}) collective-permute-start(bf16[1152,512]{1,0:T(8,128)(2,1)} %param.9), channel_id=1, source_target_pairs={{0,1},{1,0},{2,3},{3,2},{4,5},{5,4},{6,7},{7,6},{8,9},{9,8},{10,11... | collective-permute-start | bytes 3538952 | tf_op jit(solution)/shard_map/ppermute | solution.py:171
  3.8 1.7 %collective-permute-start.1 = (bf16[1152,512]{1,0:T(8,128)(2,1)}, bf16[1152,512]{1,0:T(8,128)(2,1)}, u32[]{:S(2)}, u32[]{:S(2)}) collective-permute-start(bf16[1152,512]{1,0:T(8,128)(2,1)} %param.9), channel_id=1, source_target_pairs={{1,2},{2,1},{5,6},{6,5},{9,10},{10,9},{13,14},{14,13},{17,18},{18,... | collective-permute-start | bytes 3538952 | tf_op jit(solution)/shard_map/ppermute | solution.py:171
  5.5 0.0 copy-done
  5.5 0.9 constant_dynamic-slice_fusion
  6.3 23.7 %collective-permute-done = bf16[1152,512]{1,0:T(8,128)(2,1)} collective-permute-done((bf16[1152,512]{1,0:T(8,128)(2,1)}, bf16[1152,512]{1,0:T(8,128)(2,1)}, u32[]{:S(2)}, u32[]{:S(2)}) %collective-permute-start) | collective-permute-done | bytes 1179680 | tf_op jit(solution)/shard_map/ppermute | solution.py:171
  30.0 0.7 collective-permute-start.3
  30.8 7.2 %collective-permute-start.4 = (bf16[1152,256]{1,0:T(8,128)(2,1)}, bf16[1152,256]{1,0:T(8,128)(2,1)}, u32[]{:S(2)}, u32[]{:S(2)}) collective-permute-start(bf16[1152,256]{1,0:T(8,128)(2,1)} %constant_dynamic-slice_fusion), channel_id=1, source_target_pairs={{0,1},{3,2},{4,5},{7,6},{8,9},{11,10},{12,13},{15,14},{16,17},{19,... | collective-permute-start | bytes 1769480 | tf_op jit(solution)/shard_map/ppermute | solution.py:171
  38.0 0.0 copy-done.4
  38.0 0.0 collective-permute-done.1
  38.0 1.3 %collective-permute-start.2 = (bf16[1152,512]{1,0:T(8,128)(2,1)}, bf16[1152,512]{1,0:T(8,128)(2,1)}, u32[]{:S(2)}, u32[]{:S(2)}) collective-permute-start(bf16[1152,512]{1,0:T(8,128)(2,1)} %collective-permute-done.1), channel_id=1, source_target_pairs={{1,0},{2,3},{5,4},{6,7},{9,8},{10,11},{13,12},{14,15},{17,16},{18,... | collective-permute-start | bytes 3538952 | tf_op jit(solution)/shard_map/ppermute | solution.py:171
  39.3 0.0 copy-done.5
  39.4 0.7 broadcast_in_dim.9
  40.0 0.8 reshape.12.rows_ref.refs_8_
  40.8 0.7 broadcast_in_dim.10
  41.5 0.8 reshape.13.cols_ref.refs_9_
  42.3 1.8 %fusion.6 = f32[256,512]{1,0:T(8,128)S(1)} fusion(bf16[1152,512]{1,0:T(8,128)(2,1)} %param.9, bf16[4608,256]{1,0:T(8,128)(2,1)S(1)} %copy-done, s32[]{:T(128)S(6)} %select_n.27), kind=kOutput, calls=%fused_computation.8 | convolution fusion | flops 301989888 | bytes 2293764 | tf_op jit(solution)/shard_map/dot_general | solution.py:51
  44.1 4.8 %collective-permute-done.4 = bf16[1152,256]{1,0:T(8,128)(2,1)} collective-permute-done((bf16[1152,256]{1,0:T(8,128)(2,1)}, bf16[1152,256]{1,0:T(8,128)(2,1)}, u32[]{:S(2)}, u32[]{:S(2)}) %collective-permute-start.4) | collective-permute-done | bytes 589856 | tf_op jit(solution)/shard_map/ppermute | solution.py:171
  48.9 0.0 collective-permute-done.3
  48.9 1.6 %fusion.16 = f32[256,512]{1,0:T(8,128)S(1)} fusion(bf16[1152,256]{1,0:T(8,128)(2,1)} %collective-permute-done.4, bf16[1152,512]{1,0:T(8,128)(2,1)S(1)} %collective-permute-done.3), kind=kOutput, calls=%fused_computation.29 | convolution fusion | flops 301989888 | bytes 2293760 | tf_op jit(solution)/shard_map/dot_general | solution.py:51
  50.5 1.3 %collective-permute-start.5 = (f32[256,512]{1,0:T(8,128)S(1)}, f32[256,512]{1,0:T(8,128)S(1)}, u32[]{:S(2)}, u32[]{:S(2)}) collective-permute-start(f32[256,512]{1,0:T(8,128)S(1)} %fusion.16), channel_id=1, source_target_pairs={{1,0},{2,3},{5,4},{6,7},{9,8},{10,11},{13,12},{14,15},{17,16},{18,... | collective-permute-start | bytes 1572872 | tf_op jit(solution)/shard_map/ppermute | solution.py:171
  51.8 1.8 %convolution_add_fusion.1 = f32[256,512]{1,0:T(8,128)S(1)} fusion(f32[256,512]{1,0:T(8,128)S(1)} %fusion.6, bf16[1152,512]{1,0:T(8,128)(2,1)} %collective-permute-done, bf16[4608,256]{1,0:T(8,128)(2,1)S(1)} %copy-done, s32[]{:T(128)S(6)} %select_n.28), kind=kOutput, calls=%fused_computation.2 | convolution fusion | flops 302120960 | bytes 2818052 | tf_op jit(solution)/shard_map/dot_general | solution.py:51
  53.6 0.0 copy-start.3
  53.6 1.6 %fusion.15 = f32[256,512]{1,0:T(8,128)S(1)} fusion(bf16[1152,256]{1,0:T(8,128)(2,1)} %constant_dynamic-slice_fusion, bf16[1152,512]{1,0:T(8,128)(2,1)S(1)} %collective-permute-done.3), kind=kOutput, calls=%fused_computation.28 | convolution fusion | flops 301989888 | bytes 2293760 | tf_op jit(solution)/shard_map/dot_general | solution.py:51
  55.3 0.0 copy-start.1
  55.3 0.0 copy-start.2
  55.3 13.8 %collective-permute-done.2 = bf16[1152,512]{1,0:T(8,128)(2,1)} collective-permute-done((bf16[1152,512]{1,0:T(8,128)(2,1)}, bf16[1152,512]{1,0:T(8,128)(2,1)}, u32[]{:S(2)}, u32[]{:S(2)}) %collective-permute-start.2) | collective-permute-done | bytes 1179680 | tf_op jit(solution)/shard_map/ppermute | solution.py:171
  69.1 8.5 %collective-permute-done.5 = f32[256,512]{1,0:T(8,128)S(1)} collective-permute-done((f32[256,512]{1,0:T(8,128)S(1)}, f32[256,512]{1,0:T(8,128)S(1)}, u32[]{:S(2)}, u32[]{:S(2)}) %collective-permute-start.5) | collective-permute-done | bytes 524320 | tf_op jit(solution)/shard_map/ppermute | solution.py:171
  77.6 2.2 %fusion.2.m_ref = f32[256,512]{1,0:T(8,128)S(1)} fusion(f32[256,512]{1,0:T(8,128)S(1)} %collective-permute-done.5, f32[256,512]{1,0:T(8,128)S(1)} %fusion.15, f32[256,512]{1,0:T(8,128)S(1)} %convolution_add_fusion.1, bf16[1152,512]{1,0:T(8,128)(2,1)} %collective-permute-done.1, bf16[1152,512]{1,0:T(8,128)(2,1)} %collective-permute-done.2, ...), kind=kOutput, calls=%fused_computation.4 | convolution fusion | flops 303235072 | bytes 5570564 | tf_op jit(solution)/shard_map/dot_general | solution.py:51
  79.9 0.8 shard_map.95.bands_ref.refs_0_
  80.7 0.1 collective-permute-start.10
  80.8 2.5 %collective-permute-start.11 = (f32[64,128]{1,0:T(8,128)S(1)}, f32[64,128]{1,0:T(8,128)S(1)}, u32[]{:S(2)}, u32[]{:S(2)}) collective-permute-start(f32[64,128]{1,0:T(8,128)S(1)} %shard_map.95.bands_ref.refs_0_), channel_id=1, source_target_pairs={{0,24},{4,28},{8,16},{12,20},{16,8},{20,12},{24,0},{28,4},{1,25},{... | collective-permute-start | bytes 98312 | tf_op jit(solution)/shard_map/ppermute | solution.py:145
  83.3 1.4 %collective-permute-start.12 = (f32[64,128]{1,0:T(8,128)S(1)}, f32[64,128]{1,0:T(8,128)S(1)}, u32[]{:S(2)}, u32[]{:S(2)}) collective-permute-start(f32[64,128]{1,0:T(8,128)S(1)} %shard_map.95.bands_ref.refs_0_), channel_id=1, source_target_pairs={{0,28},{4,24},{8,20},{12,16},{16,12},{20,8},{24,4},{28,0},{1,29},{... | collective-permute-start | bytes 98312 | tf_op jit(solution)/shard_map/ppermute | solution.py:145
  84.7 0.0 collective-permute-start.6
  84.7 1.5 %collective-permute-start.7 = (f32[64,128]{1,0:T(8,128)S(1)}, f32[64,128]{1,0:T(8,128)S(1)}, u32[]{:S(2)}, u32[]{:S(2)}) collective-permute-start(f32[64,128]{1,0:T(8,128)S(1)} %shard_map.95.bands_ref.refs_0_), channel_id=1, source_target_pairs={{0,8},{4,12},{8,0},{12,4},{16,24},{20,28},{24,16},{28,20},{1,9},{5... | collective-permute-start | bytes 98312 | tf_op jit(solution)/shard_map/ppermute | solution.py:145
  86.2 0.0 collective-permute-done.10.refs_5_
  86.2 0.4 collective-permute-start.8
  86.5 0.0 collective-permute-done.11.refs_6_
  86.5 0.7 collective-permute-start.9
  87.2 1.7 %shard_map.96 = f32[256,512]{1,0:T(8,128)} custom-call(f32[256,512]{1,0:T(8,128)S(1)} %fusion.2.m_ref, f32[64,128]{1,0:T(8,128)S(1)} %shard_map.95.bands_ref.refs_0_, s32[4,512]{1,0:T(4,128)S(1)} %reshape.12.rows_ref.refs_8_, s32[4,512]{1,0:T(4,128)S(1)} %reshape.13.cols_ref.refs_9_, bf16[512,128]{1,0:T(8,128)(2,1)S(1)} %copy-done.2, ...), custom_call_target="tpu_custom_call" | custom-call | flops 400000000 | bytes 4000000 | tf_op jit(solution)/shard_map/pallas_call | solution.py:126
  89.0 0.0 collective-permute-done.12.refs_7_
  89.0 0.0 collective-permute-done.6.refs_1_
  89.0 0.0 collective-permute-done.7.refs_2_
  89.0 0.5 collective-permute-done.8.refs_3_
  89.5 0.9 %collective-permute-done.9.refs_4_ = f32[64,128]{1,0:T(8,128)S(1)} collective-permute-done((f32[64,128]{1,0:T(8,128)S(1)}, f32[64,128]{1,0:T(8,128)S(1)}, u32[]{:S(2)}, u32[]{:S(2)}) %collective-permute-start.9) | collective-permute-done | bytes 32800 | tf_op jit(solution)/shard_map/ppermute | solution.py:145
  90.5 1.7 %shard_map.97 = bf16[256,512]{1,0:T(8,128)(2,1)} custom-call(f32[64,128]{1,0:T(8,128)S(1)} %shard_map.95.bands_ref.refs_0_, f32[64,128]{1,0:T(8,128)S(1)} %collective-permute-done.6.refs_1_, f32[64,128]{1,0:T(8,128)S(1)} %collective-permute-done.7.refs_2_, f32[64,128]{1,0:T(8,128)S(1)} %collective-permute-done.8.refs_3_, ...), custom_call_target="tpu_custom_call" | custom-call | flops 400000000 | bytes 4000000 | tf_op jit(solution)/shard_map/pallas_call | solution.py:126
  (5 shorter events, 0.0 us)
Async XLA Ops:
  0.6 4.8 %copy-start = (bf16[4608,256]{1,0:T(8,128)(2,1)S(1)}, bf16[4608,256]{1,0:T(8,128)(2,1)}, u32[]{:S(2)}) copy-start(bf16[4608,256]{1,0:T(8,128)(2,1)} %param.8) | copy-start | bytes 7077892
  0.6 37.4 %copy-start.4 = (s32[4,8]{1,0:T(4,128)S(1)}, s32[4,8]{1,0:T(4,128)}, u32[]{:S(2)}) copy-start(s32[4,8]{1,0:T(4,128)} %param.11) | copy-start | bytes 388
  0.7 38.7 %copy-start.5 = (s32[4,8]{1,0:T(4,128)S(1)}, s32[4,8]{1,0:T(4,128)}, u32[]{:S(2)}) copy-start(s32[4,8]{1,0:T(4,128)} %param.12) | copy-start | bytes 388
  0.7 29.4 %collective-permute-start = (bf16[1152,512]{1,0:T(8,128)(2,1)}, bf16[1152,512]{1,0:T(8,128)(2,1)}, u32[]{:S(2)}, u32[]{:S(2)}) collective-permute-start(bf16[1152,512]{1,0:T(8,128)(2,1)} %param.9), channel_id=1, source_target_pairs={{0,1},{1,0},{2,3},{3,2},{4,5},{5,4},{6,7},{7,6},{8,9},{9,8},{10,11... | collective-permute-start | bytes 3538952 | tf_op jit(solution)/shard_map/ppermute | solution.py:171
  3.8 34.3 %collective-permute-start.1 = (bf16[1152,512]{1,0:T(8,128)(2,1)}, bf16[1152,512]{1,0:T(8,128)(2,1)}, u32[]{:S(2)}, u32[]{:S(2)}) collective-permute-start(bf16[1152,512]{1,0:T(8,128)(2,1)} %param.9), channel_id=1, source_target_pairs={{1,2},{2,1},{5,6},{6,5},{9,10},{10,9},{13,14},{14,13},{17,18},{18,... | collective-permute-start | bytes 3538952 | tf_op jit(solution)/shard_map/ppermute | solution.py:171
  30.0 18.9 %collective-permute-start.3 = (bf16[1152,512]{1,0:T(8,128)(2,1)}, bf16[1152,512]{1,0:T(8,128)(2,1)S(1)}, u32[]{:S(2)}, u32[]{:S(2)}) collective-permute-start(bf16[1152,512]{1,0:T(8,128)(2,1)} %collective-permute-done), channel_id=1, source_target_pairs={{1,2},{2,1},{5,6},{6,5},{9,10},{10,9},{13,14},{14,13},{17,18},{18,... | collective-permute-start | bytes 3538952 | tf_op jit(solution)/shard_map/ppermute | solution.py:171
  30.8 18.1 %collective-permute-start.4 = (bf16[1152,256]{1,0:T(8,128)(2,1)}, bf16[1152,256]{1,0:T(8,128)(2,1)}, u32[]{:S(2)}, u32[]{:S(2)}) collective-permute-start(bf16[1152,256]{1,0:T(8,128)(2,1)} %constant_dynamic-slice_fusion), channel_id=1, source_target_pairs={{0,1},{3,2},{4,5},{7,6},{8,9},{11,10},{12,13},{15,14},{16,17},{19,... | collective-permute-start | bytes 1769480 | tf_op jit(solution)/shard_map/ppermute | solution.py:171
  38.0 31.1 %collective-permute-start.2 = (bf16[1152,512]{1,0:T(8,128)(2,1)}, bf16[1152,512]{1,0:T(8,128)(2,1)}, u32[]{:S(2)}, u32[]{:S(2)}) collective-permute-start(bf16[1152,512]{1,0:T(8,128)(2,1)} %collective-permute-done.1), channel_id=1, source_target_pairs={{1,0},{2,3},{5,4},{6,7},{9,8},{10,11},{13,12},{14,15},{17,16},{18,... | collective-permute-start | bytes 3538952 | tf_op jit(solution)/shard_map/ppermute | solution.py:171
  50.5 27.1 %collective-permute-start.5 = (f32[256,512]{1,0:T(8,128)S(1)}, f32[256,512]{1,0:T(8,128)S(1)}, u32[]{:S(2)}, u32[]{:S(2)}) collective-permute-start(f32[256,512]{1,0:T(8,128)S(1)} %fusion.16), channel_id=1, source_target_pairs={{1,0},{2,3},{5,4},{6,7},{9,8},{10,11},{13,12},{14,15},{17,16},{18,... | collective-permute-start | bytes 1572872 | tf_op jit(solution)/shard_map/ppermute | solution.py:171
  53.6 24.0 %copy-start.3 = (f32[1,256,512]{2,1,0:T(8,128)S(1)}, f32[1,256,512]{2,1,0:T(8,128)}, u32[]{:S(2)}) copy-start(f32[1,256,512]{2,1,0:T(8,128)} %param.10) | copy-start | bytes 1572868
  55.3 24.6 %copy-start.1 = (bf16[2,256,256]{2,1,0:T(8,128)(2,1)S(1)}, bf16[2,256,256]{2,1,0:T(8,128)(2,1)}, u32[]{:S(2)}) copy-start(bf16[2,256,256]{2,1,0:T(8,128)(2,1)} %constant.44.clone.row_basis_ref.column_basis_ref.refs_11_.refs_12_) | copy-start | bytes 786436
  55.3 24.6 %copy-start.2 = (bf16[512,128]{1,0:T(8,128)(2,1)S(1)}, bf16[512,128]{1,0:T(8,128)(2,1)}, u32[]{:S(2)}) copy-start(bf16[512,128]{1,0:T(8,128)(2,1)} %constant.43.clone.fold_ref.refs_10_) | copy-start | bytes 393220
  80.7 5.5 %collective-permute-start.10 = (f32[64,128]{1,0:T(8,128)S(1)}, f32[64,128]{1,0:T(8,128)S(1)}, u32[]{:S(2)}, u32[]{:S(2)}) collective-permute-start(f32[64,128]{1,0:T(8,128)S(1)} %shard_map.95.bands_ref.refs_0_), channel_id=1, source_target_pairs={{0,20},{4,16},{8,28},{12,24},{16,4},{20,0},{24,12},{28,8},{1,21},{... | collective-permute-start | bytes 98312 | tf_op jit(solution)/shard_map/ppermute | solution.py:145
  80.8 5.7 %collective-permute-start.11 = (f32[64,128]{1,0:T(8,128)S(1)}, f32[64,128]{1,0:T(8,128)S(1)}, u32[]{:S(2)}, u32[]{:S(2)}) collective-permute-start(f32[64,128]{1,0:T(8,128)S(1)} %shard_map.95.bands_ref.refs_0_), channel_id=1, source_target_pairs={{0,24},{4,28},{8,16},{12,20},{16,8},{20,12},{24,0},{28,4},{1,25},{... | collective-permute-start | bytes 98312 | tf_op jit(solution)/shard_map/ppermute | solution.py:145
  83.3 5.6 %collective-permute-start.12 = (f32[64,128]{1,0:T(8,128)S(1)}, f32[64,128]{1,0:T(8,128)S(1)}, u32[]{:S(2)}, u32[]{:S(2)}) collective-permute-start(f32[64,128]{1,0:T(8,128)S(1)} %shard_map.95.bands_ref.refs_0_), channel_id=1, source_target_pairs={{0,28},{4,24},{8,20},{12,16},{16,12},{20,8},{24,4},{28,0},{1,29},{... | collective-permute-start | bytes 98312 | tf_op jit(solution)/shard_map/ppermute | solution.py:145
  84.7 4.3 %collective-permute-start.6 = (f32[64,128]{1,0:T(8,128)S(1)}, f32[64,128]{1,0:T(8,128)S(1)}, u32[]{:S(2)}, u32[]{:S(2)}) collective-permute-start(f32[64,128]{1,0:T(8,128)S(1)} %shard_map.95.bands_ref.refs_0_), channel_id=1, source_target_pairs={{0,4},{4,0},{8,12},{12,8},{16,20},{20,16},{24,28},{28,24},{1,5},{5... | collective-permute-start | bytes 98312 | tf_op jit(solution)/shard_map/ppermute | solution.py:145
  84.7 4.3 %collective-permute-start.7 = (f32[64,128]{1,0:T(8,128)S(1)}, f32[64,128]{1,0:T(8,128)S(1)}, u32[]{:S(2)}, u32[]{:S(2)}) collective-permute-start(f32[64,128]{1,0:T(8,128)S(1)} %shard_map.95.bands_ref.refs_0_), channel_id=1, source_target_pairs={{0,8},{4,12},{8,0},{12,4},{16,24},{20,28},{24,16},{28,20},{1,9},{5... | collective-permute-start | bytes 98312 | tf_op jit(solution)/shard_map/ppermute | solution.py:145
  86.2 3.3 %collective-permute-start.8 = (f32[64,128]{1,0:T(8,128)S(1)}, f32[64,128]{1,0:T(8,128)S(1)}, u32[]{:S(2)}, u32[]{:S(2)}) collective-permute-start(f32[64,128]{1,0:T(8,128)S(1)} %shard_map.95.bands_ref.refs_0_), channel_id=1, source_target_pairs={{0,12},{4,8},{8,4},{12,0},{16,28},{20,24},{24,20},{28,16},{1,13},{... | collective-permute-start | bytes 98312 | tf_op jit(solution)/shard_map/ppermute | solution.py:145
  86.5 3.9 %collective-permute-start.9 = (f32[64,128]{1,0:T(8,128)S(1)}, f32[64,128]{1,0:T(8,128)S(1)}, u32[]{:S(2)}, u32[]{:S(2)}) collective-permute-start(f32[64,128]{1,0:T(8,128)S(1)} %shard_map.95.bands_ref.refs_0_), channel_id=1, source_target_pairs={{0,16},{4,20},{8,24},{12,28},{16,0},{20,4},{24,8},{28,12},{1,17},{... | collective-permute-start | bytes 98312 | tf_op jit(solution)/shard_map/ppermute | solution.py:145

commit v2 on v1

--- a/solution.py
+++ b/solution.py
@@ -108,18 +108,14 @@
     )
 
 
-def update_kernel(*refs):
-    *part_refs, rows_ref, cols_ref, fold_ref, row_basis_ref, column_basis_ref, out_ref = refs
-    parts = [ref[...] for ref in part_refs]
+def update_kernel(parts_ref, rows_ref, cols_ref, fold_ref, row_basis_ref, column_basis_ref, out_ref):
+    count = rows_ref.shape[0] * band
+    parts = [parts_ref[i : i + count] for i in range(0, parts_ref.shape[0], count)]
+    while len(parts) > 1:
+        parts = [sum(parts[i : i + 2]) for i in range(0, len(parts), 2)]
     out_ref[...] = lifted(
-        pair_sum(parts), rows_ref, cols_ref, fold_ref, row_basis_ref, column_basis_ref
+        parts[0], rows_ref, cols_ref, fold_ref, row_basis_ref, column_basis_ref
     ).astype(out_ref.dtype)
-
-
-def pair_sum(parts):
-    while len(parts) > 1:
-        parts = [a + b for a, b in zip(parts[::2], parts[1::2])]
-    return parts[0]
 
 
 def call(kernel, shape, dtype, *operands):
@@ -133,19 +129,10 @@
     )(*operands)
 
 
-def spread_sum(x, axis):
+def spread(x, axis):
     size = lax.axis_size(axis)
-    if size & (size - 1):
-        return [lax.psum(x, axis)]
-    stride, parts = 1, [x]
-    while stride < size:
-        count = min(8, size // stride)
-        x = pair_sum(parts)
-        parts = [x] + [
-            lax.ppermute(x, axis, [(i, i ^ (stride * k)) for i in range(size)]) for k in range(1, count)
-        ]
-        stride *= count
-    return parts
+    copies = jnp.broadcast_to(x[None], (size,) + x.shape).reshape((size * x.shape[0],) + x.shape[1:])
+    return lax.all_to_all(copies, axis, 0, 0, tiled=True)
 
 
 def product(hidden_rows, grad_rows):
@@ -204,9 +191,9 @@
     m = decay_rate * momentum[0] + gradient
     folded_shape = (row_count // steps, col_count // steps)
     bands = call(bands_kernel, folded_shape, jnp.float32, m, *tables)
-    parts = spread_sum(bands, "rep")
+    parts = spread(bands, "rep")
     momentum_out = call(remove_kernel, m.shape, jnp.float32, m, bands, *tables)
-    update = call(update_kernel, m.shape, jnp.bfloat16, *parts, *tables)
+    update = call(update_kernel, m.shape, jnp.bfloat16, parts, *tables)
     return (momentum_out[None], update)
 
 

time: 92.6 us -> 94.5 us (1.021)
  starting transfers between devices: 21.8 us -> 18.2 us
  waiting for transfers between devices: 52.4 us -> 55.6 us
  local copies, waits for them, and re-layouts: 3.83 us -> 5.54 us
    ppermute x7 -> x0, starting transfers between devices: 6.47 us -> none  [spread_sum(): lax.ppermute(x, axis, [(i, i ^ stride * k) for i in range(size)])]
    all_to_all x0 -> x1, waiting for transfers between devices: none -> 4.29 us  [spread(): return lax.all_to_all(copies, axis, 0, 0, tiled=True)]
    all_to_all x0 -> x1, starting transfers between devices: none -> 3.72 us  [spread(): return lax.all_to_all(copies, axis, 0, 0, tiled=True)]
    unnamed x12 -> x16, local copies, waits for them, and re-layouts: 0.04 us -> 1.84 us
    ppermute x7 -> x0, waiting for transfers between devices: 1.5 us -> none  [spread_sum(): lax.ppermute(x, axis, [(i, i ^ stride * k) for i in range(size)])]
  transfers between devices with their start and end apart: 13 -> 7, of which waited for: 6 -> 5; matrix products, arithmetic and copies ran while one was open for 12% -> 11% of each run, Pallas kernels for 2% -> 2%
where the time goes in v2:
time: 94.5 us; the launch traced here: 93.9 us
  waiting for transfers between devices  55.6 us (59%)
  starting transfers between devices  18.2 us (19%)
  matrix products  9.42 us (10%)
  local copies, waits for them, and re-layouts  5.54 us (6%)
  Pallas kernels  4.21 us (4%)
    ppermute x6, waiting for transfers between devices, send(): return lax.ppermute(x, 'tp', perm)  51.3 us
    ppermute x6, starting transfers between devices, send(): return lax.ppermute(x, 'tp', perm)  14.5 us
    dot_general x5, matrix products, dot(): lax.dot_general(a, b, (dims, ((), ())), preferred_element_type=jnp.float32)  9.42 us
    all_to_all x1, waiting for transfers between devices, spread(): return lax.all_to_all(copies, axis, 0, 0, tiled=True)  4.29 us
    pallas_call x3, Pallas kernels, call(): pl.pallas_call(kernel, out_shape=jax.ShapeDtypeStruct(shape, dtype), comp...  4.21 us
    all_to_all x1, starting transfers between devices, spread(): return lax.all_to_all(copies, axis, 0, 0, tiled=True)  3.72 us
  transfers between devices with their start and end apart: 7, of which 5 were waited for; matrix products, arithmetic and copies ran while one was open for 11% of the time, Pallas kernels for 2%

profile of v2, /device:TPU:0, one launch (start us, length us, event | category | flops | bytes accessed | tf_op | source)
XLA Modules:
  0.0 93.9 jit_solution(9404137442737803700)
XLA Ops:
  0.6 0.0 copy-start
  0.6 0.0 copy-start.6
  0.7 0.0 copy-start.7
  0.7 3.1 %collective-permute-start = (bf16[1152,512]{1,0:T(8,128)(2,1)}, bf16[1152,512]{1,0:T(8,128)(2,1)}, u32[]{:S(2)}, u32[]{:S(2)}) collective-permute-start(bf16[1152,512]{1,0:T(8,128)(2,1)} %param.9), channel_id=1, source_target_pairs={{0,1},{1,0},{2,3},{3,2},{4,5},{5,4},{6,7},{7,6},{8,9},{9,8},{10,11... | collective-permute-start | bytes 3538952 | tf_op jit(solution)/shard_map/ppermute | solution.py:158
  3.8 1.7 %collective-permute-start.1 = (bf16[1152,512]{1,0:T(8,128)(2,1)}, bf16[1152,512]{1,0:T(8,128)(2,1)}, u32[]{:S(2)}, u32[]{:S(2)}) collective-permute-start(bf16[1152,512]{1,0:T(8,128)(2,1)} %param.9), channel_id=1, source_target_pairs={{1,2},{2,1},{5,6},{6,5},{9,10},{10,9},{13,14},{14,13},{17,18},{18,... | collective-permute-start | bytes 3538952 | tf_op jit(solution)/shard_map/ppermute | solution.py:158
  5.4 0.0 copy-done
  5.5 24.5 %collective-permute-done = bf16[1152,512]{1,0:T(8,128)(2,1)} collective-permute-done((bf16[1152,512]{1,0:T(8,128)(2,1)}, bf16[1152,512]{1,0:T(8,128)(2,1)}, u32[]{:S(2)}, u32[]{:S(2)}) %collective-permute-start) | collective-permute-done | bytes 1179680 | tf_op jit(solution)/shard_map/ppermute | solution.py:158
  30.0 1.7 %collective-permute-start.3 = (bf16[1152,512]{1,0:T(8,128)(2,1)}, bf16[1152,512]{1,0:T(8,128)(2,1)}, u32[]{:S(2)}, u32[]{:S(2)}) collective-permute-start(bf16[1152,512]{1,0:T(8,128)(2,1)} %collective-permute-done), channel_id=1, source_target_pairs={{1,2},{2,1},{5,6},{6,5},{9,10},{10,9},{13,14},{14,13},{17,18},{18,... | collective-permute-start | bytes 3538952 | tf_op jit(solution)/shard_map/ppermute | solution.py:158
  31.7 5.5 %collective-permute-start.4 = (bf16[1152,256]{1,0:T(8,128)(2,1)S(1)}, bf16[1152,256]{1,0:T(8,128)(2,1)S(1)}, u32[]{:S(2)}, u32[]{:S(2)}) collective-permute-start(bf16[1152,256]{1,0:T(8,128)(2,1)S(1)} %constant_dynamic-slice_fusion), channel_id=1, source_target_pairs={{0,1},{3,2},{4,5},{7,6},{8,9},{11,10},{12,13},{15,14},{16,17},{19,... | collective-permute-start | bytes 1769480 | tf_op jit(solution)/shard_map/ppermute | solution.py:158
  37.2 0.0 copy-done.6
  37.2 0.0 collective-permute-done.1
  37.2 1.3 %collective-permute-start.2 = (bf16[1152,512]{1,0:T(8,128)(2,1)}, bf16[1152,512]{1,0:T(8,128)(2,1)}, u32[]{:S(2)}, u32[]{:S(2)}) collective-permute-start(bf16[1152,512]{1,0:T(8,128)(2,1)} %collective-permute-done.1), channel_id=1, source_target_pairs={{1,0},{2,3},{5,4},{6,7},{9,8},{10,11},{13,12},{14,15},{17,16},{18,... | collective-permute-start | bytes 3538952 | tf_op jit(solution)/shard_map/ppermute | solution.py:158
  38.5 0.0 copy-done.7
  38.6 0.7 broadcast_in_dim.15
  39.3 0.8 reshape.17.rows_ref
  40.1 0.7 broadcast_in_dim.16
  40.7 0.8 reshape.18.cols_ref
  41.5 1.8 %fusion.6 = f32[256,512]{1,0:T(8,128)S(1)} fusion(bf16[1152,512]{1,0:T(8,128)(2,1)} %param.9, bf16[4608,256]{1,0:T(8,128)(2,1)S(1)} %copy-done, s32[]{:T(128)S(6)} %select_n.27), kind=kOutput, calls=%fused_computation.8 | convolution fusion | flops 301989888 | bytes 2293764 | tf_op jit(solution)/shard_map/dot_general | solution.py:51
  43.3 5.3 %collective-permute-done.4 = bf16[1152,256]{1,0:T(8,128)(2,1)S(1)} collective-permute-done((bf16[1152,256]{1,0:T(8,128)(2,1)S(1)}, bf16[1152,256]{1,0:T(8,128)(2,1)S(1)}, u32[]{:S(2)}, u32[]{:S(2)}) %collective-permute-start.4) | collective-permute-done | bytes 589856 | tf_op jit(solution)/shard_map/ppermute | solution.py:158
  48.6 0.0 collective-permute-done.3
  48.6 1.8 %fusion.16 = f32[256,512]{1,0:T(8,128)S(1)} fusion(bf16[1152,256]{1,0:T(8,128)(2,1)S(1)} %collective-permute-done.4, bf16[1152,512]{1,0:T(8,128)(2,1)} %collective-permute-done.3), kind=kOutput, calls=%fused_computation.29 | convolution fusion | flops 301989888 | bytes 2293760 | tf_op jit(solution)/shard_map/dot_general | solution.py:51
  50.4 1.3 %collective-permute-start.5 = (f32[256,512]{1,0:T(8,128)S(1)}, f32[256,512]{1,0:T(8,128)S(1)}, u32[]{:S(2)}, u32[]{:S(2)}) collective-permute-start(f32[256,512]{1,0:T(8,128)S(1)} %fusion.16), channel_id=1, source_target_pairs={{1,0},{2,3},{5,4},{6,7},{9,8},{10,11},{13,12},{14,15},{17,16},{18,... | collective-permute-start | bytes 1572872 | tf_op jit(solution)/shard_map/ppermute | solution.py:158
  51.7 1.8 %convolution_add_fusion.1 = f32[256,512]{1,0:T(8,128)S(1)} fusion(f32[256,512]{1,0:T(8,128)S(1)} %fusion.6, bf16[1152,512]{1,0:T(8,128)(2,1)} %collective-permute-done, bf16[4608,256]{1,0:T(8,128)(2,1)S(1)} %copy-done, s32[]{:T(128)S(6)} %select_n.28), kind=kOutput, calls=%fused_computation.2 | convolution fusion | flops 302120960 | bytes 2818052 | tf_op jit(solution)/shard_map/dot_general | solution.py:51
  53.5 0.0 copy-start.5
  53.5 1.8 %fusion.15 = f32[256,512]{1,0:T(8,128)S(1)} fusion(bf16[1152,256]{1,0:T(8,128)(2,1)S(1)} %constant_dynamic-slice_fusion, bf16[1152,512]{1,0:T(8,128)(2,1)} %collective-permute-done.3), kind=kOutput, calls=%fused_computation.28 | convolution fusion | flops 301989888 | bytes 2293760 | tf_op jit(solution)/shard_map/dot_general | solution.py:51
  55.4 0.0 copy-start.1
  55.4 0.0 copy-start.2
  55.4 13.0 %collective-permute-done.2 = bf16[1152,512]{1,0:T(8,128)(2,1)} collective-permute-done((bf16[1152,512]{1,0:T(8,128)(2,1)}, bf16[1152,512]{1,0:T(8,128)(2,1)}, u32[]{:S(2)}, u32[]{:S(2)}) %collective-permute-start.2) | collective-permute-done | bytes 1179680 | tf_op jit(solution)/shard_map/ppermute | solution.py:158
  68.4 8.5 %collective-permute-done.5 = f32[256,512]{1,0:T(8,128)S(1)} collective-permute-done((f32[256,512]{1,0:T(8,128)S(1)}, f32[256,512]{1,0:T(8,128)S(1)}, u32[]{:S(2)}, u32[]{:S(2)}) %collective-permute-start.5) | collective-permute-done | bytes 524320 | tf_op jit(solution)/shard_map/ppermute | solution.py:158
  76.9 0.0 copy-done.5
  76.9 2.2 %fusion.2.m_ref = f32[256,512]{1,0:T(8,128)S(1)} fusion(f32[256,512]{1,0:T(8,128)S(1)} %collective-permute-done.5, f32[256,512]{1,0:T(8,128)S(1)} %fusion.15, f32[256,512]{1,0:T(8,128)S(1)} %convolution_add_fusion.1, bf16[1152,512]{1,0:T(8,128)(2,1)} %collective-permute-done.1, bf16[1152,512]{1,0:T(8,128)(2,1)} %collective-permute-done.2, ...), kind=kOutput, calls=%fused_computation.4 | convolution fusion | flops 303235072 | bytes 5570564 | tf_op jit(solution)/shard_map/dot_general | solution.py:51
  79.1 0.0 copy-done.1
  79.1 0.0 copy-done.2
  79.1 0.8 shard_map.95.bands_ref
  79.9 0.7 broadcast_in_dim.18
  80.7 3.7 %all-to-all-start = ((f32[8,64,128]{2,1,0:T(8,128)}), f32[8,64,128]{2,1,0:T(8,128)S(1)}, u32[]{:S(2)}, u32[]{:S(2)}) async-start(f32[8,64,128]{2,1,0:T(8,128)} %broadcast_in_dim.18), calls=%async_computation | async-start | bytes 524288 | tf_op jit(solution)/shard_map/all_to_all | solution.py:135
  84.4 0.0 copy-start.3
  84.4 0.9 copy-done.3
  85.3 1.7 %shard_map.96 = f32[256,512]{1,0:T(8,128)} custom-call(f32[256,512]{1,0:T(8,128)S(1)} %fusion.2.m_ref, f32[64,128]{1,0:T(8,128)S(1)} %shard_map.95.bands_ref, s32[4,512]{1,0:T(4,128)S(1)} %reshape.17.rows_ref, s32[4,512]{1,0:T(4,128)S(1)} %reshape.18.cols_ref, bf16[512,128]{1,0:T(8,128)(2,1)S(1)} %copy-done.3, bf16[2,256,256]{2,1,0:T(8,128)(2,1)S(1)} %copy-done.1, ...), custom_call_target="tpu_custom_call" | custom-call | flops 400000000 | bytes 4000000 | tf_op jit(solution)/shard_map/pallas_call | solution.py:122
  87.0 4.3 %all-to-all-done = f32[8,64,128]{2,1,0:T(8,128)S(1)} async-done(((f32[8,64,128]{2,1,0:T(8,128)}), f32[8,64,128]{2,1,0:T(8,128)S(1)}, u32[]{:S(2)}, u32[]{:S(2)}) %all-to-all-start) | async-done | bytes 262176 | tf_op jit(solution)/shard_map/all_to_all | solution.py:135
  91.3 0.0 copy-start.4
  91.3 0.9 copy-done.4
  92.2 1.6 %shard_map.97 = bf16[256,512]{1,0:T(8,128)(2,1)} custom-call(f32[512,128]{1,0:T(8,128)S(1)} %bitcast.10, s32[4,512]{1,0:T(4,128)S(1)} %reshape.17.rows_ref, s32[4,512]{1,0:T(4,128)S(1)} %reshape.18.cols_ref, bf16[512,128]{1,0:T(8,128)(2,1)S(1)} %copy-done.4, bf16[2,256,256]{2,1,0:T(8,128)(2,1)S(1)} %copy-done.1, bf16[2,256,256]{2,1,0:T(8,128)(2,1)S(1)} %copy-done.1), custom_call_target="tpu_custom_call" | custom-call | flops 400000000 | bytes 4000000 | tf_op jit(solution)/shard_map/pallas_call | solution.py:122
  (3 shorter events, 0.1 us)
Async XLA Ops:
  0.6 4.8 %copy-start = (bf16[4608,256]{1,0:T(8,128)(2,1)S(1)}, bf16[4608,256]{1,0:T(8,128)(2,1)}, u32[]{:S(2)}) copy-start(bf16[4608,256]{1,0:T(8,128)(2,1)} %param.8) | copy-start | bytes 7077892
  0.6 36.6 %copy-start.6 = (s32[4,8]{1,0:T(4,128)S(1)}, s32[4,8]{1,0:T(4,128)}, u32[]{:S(2)}) copy-start(s32[4,8]{1,0:T(4,128)} %param.11) | copy-start | bytes 388
  0.7 37.9 %copy-start.7 = (s32[4,8]{1,0:T(4,128)S(1)}, s32[4,8]{1,0:T(4,128)}, u32[]{:S(2)}) copy-start(s32[4,8]{1,0:T(4,128)} %param.12) | copy-start | bytes 388
  0.7 29.4 %collective-permute-start = (bf16[1152,512]{1,0:T(8,128)(2,1)}, bf16[1152,512]{1,0:T(8,128)(2,1)}, u32[]{:S(2)}, u32[]{:S(2)}) collective-permute-start(bf16[1152,512]{1,0:T(8,128)(2,1)} %param.9), channel_id=1, source_target_pairs={{0,1},{1,0},{2,3},{3,2},{4,5},{5,4},{6,7},{7,6},{8,9},{9,8},{10,11... | collective-permute-start | bytes 3538952 | tf_op jit(solution)/shard_map/ppermute | solution.py:158
  3.8 33.5 %collective-permute-start.1 = (bf16[1152,512]{1,0:T(8,128)(2,1)}, bf16[1152,512]{1,0:T(8,128)(2,1)}, u32[]{:S(2)}, u32[]{:S(2)}) collective-permute-start(bf16[1152,512]{1,0:T(8,128)(2,1)} %param.9), channel_id=1, source_target_pairs={{1,2},{2,1},{5,6},{6,5},{9,10},{10,9},{13,14},{14,13},{17,18},{18,... | collective-permute-start | bytes 3538952 | tf_op jit(solution)/shard_map/ppermute | solution.py:158
  30.0 18.6 %collective-permute-start.3 = (bf16[1152,512]{1,0:T(8,128)(2,1)}, bf16[1152,512]{1,0:T(8,128)(2,1)}, u32[]{:S(2)}, u32[]{:S(2)}) collective-permute-start(bf16[1152,512]{1,0:T(8,128)(2,1)} %collective-permute-done), channel_id=1, source_target_pairs={{1,2},{2,1},{5,6},{6,5},{9,10},{10,9},{13,14},{14,13},{17,18},{18,... | collective-permute-start | bytes 3538952 | tf_op jit(solution)/shard_map/ppermute | solution.py:158
  31.7 16.9 %collective-permute-start.4 = (bf16[1152,256]{1,0:T(8,128)(2,1)S(1)}, bf16[1152,256]{1,0:T(8,128)(2,1)S(1)}, u32[]{:S(2)}, u32[]{:S(2)}) collective-permute-start(bf16[1152,256]{1,0:T(8,128)(2,1)S(1)} %constant_dynamic-slice_fusion), channel_id=1, source_target_pairs={{0,1},{3,2},{4,5},{7,6},{8,9},{11,10},{12,13},{15,14},{16,17},{19,... | collective-permute-start | bytes 1769480 | tf_op jit(solution)/shard_map/ppermute | solution.py:158
  37.2 31.1 %collective-permute-start.2 = (bf16[1152,512]{1,0:T(8,128)(2,1)}, bf16[1152,512]{1,0:T(8,128)(2,1)}, u32[]{:S(2)}, u32[]{:S(2)}) collective-permute-start(bf16[1152,512]{1,0:T(8,128)(2,1)} %collective-permute-done.1), channel_id=1, source_target_pairs={{1,0},{2,3},{5,4},{6,7},{9,8},{10,11},{13,12},{14,15},{17,16},{18,... | collective-permute-start | bytes 3538952 | tf_op jit(solution)/shard_map/ppermute | solution.py:158
  50.4 26.5 %collective-permute-start.5 = (f32[256,512]{1,0:T(8,128)S(1)}, f32[256,512]{1,0:T(8,128)S(1)}, u32[]{:S(2)}, u32[]{:S(2)}) collective-permute-start(f32[256,512]{1,0:T(8,128)S(1)} %fusion.16), channel_id=1, source_target_pairs={{1,0},{2,3},{5,4},{6,7},{9,8},{10,11},{13,12},{14,15},{17,16},{18,... | collective-permute-start | bytes 1572872 | tf_op jit(solution)/shard_map/ppermute | solution.py:158
  53.5 23.4 %copy-start.5 = (f32[1,256,512]{2,1,0:T(8,128)S(1)}, f32[1,256,512]{2,1,0:T(8,128)}, u32[]{:S(2)}) copy-start(f32[1,256,512]{2,1,0:T(8,128)} %param.10) | copy-start | bytes 1572868
  55.4 23.7 %copy-start.1 = (bf16[2,256,256]{2,1,0:T(8,128)(2,1)S(1)}, bf16[2,256,256]{2,1,0:T(8,128)(2,1)}, u32[]{:S(2)}) copy-start(bf16[2,256,256]{2,1,0:T(8,128)(2,1)} %constant.44.clone.row_basis_ref.column_basis_ref) | copy-start | bytes 786436
  55.4 23.7 %copy-start.2 = (bf16[512,128]{1,0:T(8,128)(2,1)S(1)}, bf16[512,128]{1,0:T(8,128)(2,1)}, u32[]{:S(2)}) copy-start(bf16[512,128]{1,0:T(8,128)(2,1)} %constant.43.clone.fold_ref) | copy-start | bytes 393220
  80.7 10.7 %all-to-all-start = ((f32[8,64,128]{2,1,0:T(8,128)}), f32[8,64,128]{2,1,0:T(8,128)S(1)}, u32[]{:S(2)}, u32[]{:S(2)}) async-start(f32[8,64,128]{2,1,0:T(8,128)} %broadcast_in_dim.18), calls=%async_computation | async-start | bytes 524288 | tf_op jit(solution)/shard_map/all_to_all | solution.py:135
  84.4 0.9 copy-start.3
  91.3 0.9 copy-start.4
